TPU v7x, 32 devices: a whole 2x2x4 slice. The times are simulated.
32 devices in a mesh: tm: 8 (over z, y), col: 4 (over x, core).
Axes of the slice: x: 2, y: 2, z: 4, core: 2. Of those that a mesh axis runs over, the one named last changes fastest.
Arguments:
- transition: bfloat16 [64, 256, 256], P('tm', 'col'), may hold values from -1 to 1, as said below
- drive: float32 [64, 16, 256], P('tm', 'col'), may hold values from -0.3125 to 0.3125
- smoother_gain: bfloat16 [64, 256, 256], P('tm', 'col'), may hold values from -1 to 1, as said below
- dynamics: float32 [256, 256], replicated, may hold values from -0.375 to 0.375
- initial_mean: float32 [16, 256], P('col'), may hold values from -6 to 6
Outputs:
- filtered_mean: float32 [64, 16, 256], P('tm', 'col')
- smoothed_mean: float32 [64, 16, 256], P('tm', 'col')
Inputs may be any that keep to these rules, and one draw needn't show every extreme that they name: `transition`: every step operator is a per-channel diagonal plus a dense full-rank part. `smoother_gain`: every gain is a per-channel diagonal plus a dense full-rank part.
All inputs are finite; a program needn't handle non-finite values.
Results may differ from a plain program's by a relative error of at most 0.0018.
Values may be sent and summed in bfloat16 or wider, within the bound.
A program may use at most 128 MiB of HBM per device.

v0:
```python
import jax
import jax.numpy as jnp
from jax import lax
from jax.sharding import PartitionSpec as P

highest = lax.Precision.HIGHEST


def prefix(part, axis, combine, identity, reverse):
    count = lax.axis_size(axis)
    place = lax.axis_index(axis)
    ahead = count - 1 - place if reverse else place
    gathered = jax.tree.map(lambda a: lax.all_gather(a, axis), part)
    state = jax.tree.map(lambda a, e: jnp.zeros_like(a) + jnp.asarray(e, a.dtype), part, identity)

    def one(lap, state):
        source = count - 1 - lap if reverse else lap
        return combine(
            state, jax.tree.map(lambda a: lax.dynamic_index_in_dim(a, source, 0, False), gathered)
        )

    return lax.fori_loop(0, ahead, one, state)


def widen(matrix):
    return matrix.astype(jnp.float32)


def product(left, right):
    return jnp.dot(left, right, precision=highest, preferred_element_type=jnp.float32)


def combine_pair(earlier, later):
    first_op, first_vec = earlier
    second_op, second_vec = later
    return (product(first_op, second_op), product(first_vec, second_op) + second_vec)


def right_product(whole, seed, upward):
    count = whole.shape[0]

    def turn(step, current):
        position = step + 1 if upward else count - 2 - step
        return product(current, widen(whole[position]))

    return lax.fori_loop(0, count - 1, turn, widen(seed))


def run_forward(begin, operators, pushes, keep_all):

    def forward_step(state, inputs):
        operator, push = inputs
        state = product(state, widen(operator)) + push
        return (state, state if keep_all else None)

    return lax.scan(forward_step, begin, (operators, pushes))


def run_backward(begin, gains, corrections, keep_all):

    def backward_step(state, inputs):
        gain_now, corr_now = inputs
        state = product(state, widen(gain_now)) + corr_now
        return (state, state if keep_all else None)

    return lax.scan(backward_step, begin, (gains, corrections), reverse=True)


def corrections_of(filtered, gains, dynamics):

    def correct_step(carry, inputs):
        mean_now, gain_now = inputs
        projected = product(mean_now, dynamics)
        return (carry, mean_now - product(projected, widen(gain_now)))

    _, correction = lax.scan(correct_step, jnp.float32(0.0), (filtered, gains))
    return correction


def local(transition, drive, smoother_gain, dynamics, initial_mean):
    steps_dev = transition.shape[0]
    whole_trans, whole_gains = (
        lax.all_gather(transition, "col", axis=1, tiled=True),
        lax.all_gather(smoother_gain, "col", axis=1, tiled=True),
    )
    last_device = lax.axis_index("tm") == lax.axis_size("tm") - 1
    positions = jnp.arange(steps_dev)
    keep = jnp.logical_not(jnp.logical_and(last_device, positions == steps_dev - 1))
    whole_gains = jnp.where(keep[:, None, None], whole_gains, jnp.zeros_like(whole_gains))
    block_trans = right_product(whole_trans, whole_trans[0], True)
    block_gains = right_product(whole_gains, whole_gains[steps_dev - 1], False)
    empty = jnp.zeros_like(initial_mean)
    block_drive, _ = run_forward(empty, whole_trans, drive, False)
    ident = jnp.eye(block_trans.shape[0], dtype=jnp.float32)
    prefix_op, prefix_vec = prefix(
        (block_trans, block_drive), "tm", combine_pair, (ident, empty), False
    )
    incoming = product(initial_mean, prefix_op) + prefix_vec
    _, filtered = run_forward(incoming, whole_trans, drive, True)
    correction = corrections_of(filtered, whole_gains, dynamics)
    block_corr, _ = run_backward(empty, whole_gains, correction, False)
    _, next_state = prefix((block_gains, block_corr), "tm", combine_pair, (ident, empty), True)
    _, smoothed = run_backward(next_state, whole_gains, correction, True)
    return (filtered, smoothed)


def solution(mesh):
    placed = (P("tm", "col", None), P("tm", "col", None), P("tm", "col", None), P(), P("col", None))
    return jax.shard_map(
        local,
        mesh=mesh,
        in_specs=placed,
        out_specs=(P("tm", "col", None), P("tm", "col", None)),
        check_vma=False,
    )
```

profile of v0, /device:TPU:0, one launch (start us, length us, event | category | flops | bytes accessed | tf_op | source)
XLA Modules:
  0.0 171.5 jit_solution(11463969625614131097)
XLA Ops:
  8.8 20.3 %all-gather.11.cloned.1.call-done = bf16[8,256,256]{2,1,0:T(8,128)(2,1)} async-done(((bf16[8,64,256]{2,1,0:T(8,128)(2,1)}), bf16[8,256,256]{2,1,0:T(8,128)(2,1)}) %all-gather.11.cloned.1.call-update) | async-done | bytes 1048592 | tf_op jit(solution)/shard_map/all_gather | solution.py:83
  29.0 0.9 fusion.53
  30.1 8.9 %while.120 = (s32[]{:T(128)}, f32[256,256]{0,1:T(8,128)S(1)}, bf16[8,256,256]{2,1,0:T(8,128)(2,1)}, s32[]{:T(128)}, s32[]{:T(128)}, /*index=5*/s32[]{:T(128)}) while((s32[]{:T(128)}, f32[256,256]{0,1:T(8,128)S(1)}, bf16[8,256,256]{2,1,0:T(8,128)(2,1)}, s32[]{:T(128)}, s32[]{:T(128)}, /*index=5*/s32[]{:T(128)}) %tuple.223), condition=%wide.region_1.2_spmd, body=%wide.region_0.1_spmd.sunk | while | flops 201326592 | bytes 1179763 | solution.py:46
  30.1 1.2 convolution_bitcast_fusion.13
  31.4 1.2 convolution_bitcast_fusion.13
  32.7 1.2 convolution_bitcast_fusion.13
  34.0 1.2 convolution_bitcast_fusion.13
  35.2 1.2 convolution_bitcast_fusion.13
  36.5 1.2 convolution_bitcast_fusion.13
  37.8 1.2 convolution_bitcast_fusion.13
  39.8 7.5 %all-gather.13.cloned.1.call-done = bf16[8,256,256]{2,1,0:T(8,128)(2,1)} async-done(((bf16[8,64,256]{2,1,0:T(8,128)(2,1)}), bf16[8,256,256]{2,1,0:T(8,128)(2,1)}) %all-gather.13.cloned.1.call-update) | async-done | bytes 1048592 | tf_op jit(solution)/shard_map/all_gather | solution.py:84
  47.3 1.4 broadcast_select_fusion
  48.9 8.8 %while.127 = (s32[]{:T(128)}, f32[4,256]{1,0:T(4,128)S(1)}, bf16[8,256,256]{2,1,0:T(8,128)(2,1)}, f32[8,4,256]{2,1,0:T(4,128)}, s32[]{:T(128)}, /*index=5*/s32[]{:T(128)}) while((s32[]{:T(128)}, f32[4,256]{1,0:T(4,128)S(1)}, bf16[8,256,256]{2,1,0:T(8,128)(2,1)}, f32[8,4,256]{2,1,0:T(4,128)}, s32[]{:T(128)}, ...), condition=%wide.region_3.4_spmd.clone, body=%wide.region_2.3_spmd.clone.sunk | while | flops 3147779 | bytes 152655 | solution.py:56
  48.9 1.0 fusion.113
  50.0 1.1 fusion.113
  51.1 1.1 fusion.113
  52.2 1.1 fusion.113
  53.3 1.1 fusion.113
  54.4 1.0 fusion.113
  55.5 1.1 fusion.113
  56.6 1.1 fusion.113
  57.7 30.9 %all-gather.4 = f32[8,4,256]{2,1,0:T(4,128)S(1)} all-gather(f32[1,4,256]{2,1,0:T(4,128)S(1)} %bitcast.189), channel_id=3, replica_groups=mesh['tm'=8,'col'=4] {'tm'}, dimensions={0}, use_global_device_ids=true | all-gather | bytes 36864 | tf_op jit(solution)/shard_map/all_gather | solution.py:13
  88.5 2.6 %while.123 = (s32[]{:T(128)}, f32[256,256]{0,1:T(8,128)S(1)}, bf16[8,256,256]{2,1,0:T(8,128)(2,1)S(1)}, s32[]{:T(128)}, s32[]{:T(128)}, /*index=5*/s32[]{:T(128)}, s32[]{:T(128)}) while((s32[]{:T(128)}, f32[256,256]{0,1:T(8,128)S(1)}, bf16[8,256,256]{2,1,0:T(8,128)(2,1)S(1)}, s32[]{:T(128)}, s32[]{:T(128)}, /*index=5*/s32[]{:T(128)}, ...), condition=%wide.region_9.10_spmd, body=%wide.region_8.9_spmd.sunk | while | flops 201326592 | bytes 1179775 | solution.py:46
  91.9 8.9 %all-gather.15.cloned.1.call-done = f32[2048,256]{0,1:T(8,128)} async-done(((f32[256,256]{0,1:T(8,128)}), f32[2048,256]{0,1:T(8,128)}) %all-gather.15.cloned.1.call-update) | async-done | bytes 2097168 | tf_op jit(solution)/shard_map/all_gather | solution.py:13
  100.8 1.9 %copy.12 = f32[2048,256]{1,0:T(8,128)S(1)} copy(f32[2048,256]{0,1:T(8,128)} %all-gather.15.cloned.1.call-done) | data formatting | bytes 4194304 | tf_op jit(solution)/shard_map/all_gather | solution.py:13
  103.1 8.8 %while.122 = (s32[]{:T(128)}, f32[4,256]{1,0:T(4,128)S(1)}, f32[8,4,256]{2,1,0:T(4,128)S(1)}, bf16[8,256,256]{2,1,0:T(8,128)(2,1)}, f32[8,4,256]{2,1,0:T(4,128)}, /*index=5*/s32[]{:T(128)}) while((s32[]{:T(128)}, f32[4,256]{1,0:T(4,128)S(1)}, f32[8,4,256]{2,1,0:T(4,128)S(1)}, bf16[8,256,256]{2,1,0:T(8,128)(2,1)}, f32[8,4,256]{2,1,0:T(4,128)}, ...), condition=%wide.region_7.8_spmd, body=%wide.region_6.7_spmd.sunk | while | flops 3146754 | bytes 156741 | solution.py:56
  103.1 1.1 bitcast_dynamic-update-slice_fusion.4
  104.2 1.1 bitcast_dynamic-update-slice_fusion.4
  105.3 1.1 bitcast_dynamic-update-slice_fusion.4
  106.4 1.0 bitcast_dynamic-update-slice_fusion.4
  107.5 1.1 bitcast_dynamic-update-slice_fusion.4
  108.6 1.1 bitcast_dynamic-update-slice_fusion.4
  109.7 1.1 bitcast_dynamic-update-slice_fusion.4
  110.8 1.1 bitcast_dynamic-update-slice_fusion.4
  111.9 11.0 %while.124 = (s32[]{:T(128)}, f32[8,4,256]{2,1,0:T(4,128)S(1)}, f32[8,4,256]{2,1,0:T(4,128)S(1)}, f32[256,256]{1,0:T(8,128)}, bf16[8,256,256]{2,1,0:T(8,128)(2,1)S(1)}, /*index=5*/s32[]{:T(128)}) while((s32[]{:T(128)}, f32[8,4,256]{2,1,0:T(4,128)S(1)}, f32[8,4,256]{2,1,0:T(4,128)S(1)}, f32[256,256]{1,0:T(8,128)}, ...), condition=%wide.region_11.12_spmd, body=%wide.region_10.11_spmd.sunk | while | flops 6292482 | bytes 414793 | solution.py:76
  111.9 1.1 fusion.105
  113.3 1.1 fusion.105
  114.6 1.2 fusion.105
  116.0 1.2 fusion.105
  117.4 1.2 fusion.105
  118.8 1.2 fusion.105
  120.1 1.2 fusion.105
  121.5 1.2 fusion.105
  122.9 1.6 while.128
  124.5 34.4 %all-gather.5 = f32[8,4,256]{2,1,0:T(4,128)S(1)} all-gather(f32[1,4,256]{2,1,0:T(4,128)S(1)} %bitcast.188), channel_id=5, replica_groups=mesh['tm'=8,'col'=4] {'tm'}, dimensions={0}, use_global_device_ids=true | all-gather | bytes 36864 | tf_op jit(solution)/shard_map/all_gather | solution.py:13
  158.9 1.9 %copy.14 = f32[2048,256]{1,0:T(8,128)S(1)} copy(f32[2048,256]{0,1:T(8,128)} %all-gather.17.cloned.1.call-done) | data formatting | bytes 4194304 | tf_op jit(solution)/shard_map/all_gather | solution.py:13
  160.9 1.8 %while.125 = (s32[]{:T(128)}, f32[4,256]{1,0:T(4,128)S(1)}, s32[]{:T(128)}, f32[8,256,256]{2,1,0:T(8,128)S(1)}, f32[8,4,256]{2,1,0:T(4,128)S(1)}, /*index=5*/s32[]{:T(128)}, s32[]{:T(128)}, s32[]{:T(128)}, s32[]{:T(128)}) while((s32[]{:T(128)}, f32[4,256]{1,0:T(4,128)S(1)}, s32[]{:T(128)}, f32[8,256,256]{2,1,0:T(8,128)S(1)}, ...), condition=%wide.region_15.16_spmd, body=%wide.region_14.15_spmd.sunk | while | flops 3146758 | bytes 283787 | solution.py:22
  162.7 1.6 while.126
  (124 shorter events, 13.4 us)
Async XLA Ops:
  7.2 95.6 %copy-start = (f32[4,256]{1,0:T(4,128)S(1)}, f32[4,256]{1,0:T(4,128)}, u32[]{:S(2)}) copy-start(f32[4,256]{1,0:T(4,128)} %param.27) | copy-start | bytes 12292
  7.2 21.9 %all-gather.11.cloned.1.call-start = ((), (), s32[]{:S(2)}) async-start(), calls=%async_computation | async-start | bytes 1310720 | tf_op jit(solution)/shard_map/all_gather | solution.py:83
  7.9 39.4 %all-gather.13.cloned.1.call-start = ((), (), s32[]{:S(2)}) async-start(), calls=%async_computation.1 | async-start | bytes 1310720 | tf_op jit(solution)/shard_map/all_gather | solution.py:84
  8.7 92.1 %all-gather.15.cloned.1.call-start = ((), (), s32[]{:S(2)}) async-start(), calls=%async_computation.2 | async-start | bytes 2359296 | tf_op jit(solution)/shard_map/all_gather | solution.py:13
  39.0 0.7 copy-start.2
  39.8 119.1 %all-gather.17.cloned.1.call-start = ((), (), s32[]{:S(2)}) async-start(), calls=%async_computation.3 | async-start | bytes 2359296 | tf_op jit(solution)/shard_map/all_gather | solution.py:13
  91.1 0.7 copy-start.1
  122.9 37.9 %copy-start.3 = (f32[8,4,256]{2,1,0:T(4,128)}, f32[8,4,256]{2,1,0:T(4,128)S(1)}, u32[]{:S(2)}) copy-start(f32[8,4,256]{2,1,0:T(4,128)S(1)} %get-tuple-element.1164) | copy-start | bytes 98308
  164.3 0.7 copy-start.4
Sparse Core Ops, SparseCore 0:
  9.6 19.4 all-gather.10
  30.6 16.7 all-gather.12
  49.4 51.3 all-gather.14
  102.7 49.2 all-gather.16
where the time goes:
time: 172 us
  blocking collectives  65.3 us (38%)
  matrix products  44.1 us (26%)
  waiting for transfers between devices  38.1 us (22%)
  between operations  14 us (8%)
  local copies, waits for them, and re-layouts  6.77 us (4%)
  other arithmetic  2.33 us (1%)
    all_gather x2, blocking collectives, prefix(): gathered = jax.tree.map(lambda a: lax.all_gather(a, axis), part)  65.3 us
    dot_general x70, matrix products, product(): jnp.dot(left, right, precision=highest, preferred_element_type=jnp.float32)  44.1 us
    all_gather x1, waiting for transfers between devices, local(): lax.all_gather(transition, 'col', axis=1, tiled=True)  20.3 us
    all_gather x2, waiting for transfers between devices, prefix(): gathered = jax.tree.map(lambda a: lax.all_gather(a, axis), part)  8.9 us
    all_gather x1, waiting for transfers between devices, local(): lax.all_gather(smoother_gain, 'col', axis=1, tiled=True)  7.54 us
    all_gather x2, local copies, waits for them, and re-layouts, prefix(): gathered = jax.tree.map(lambda a: lax.all_gather(a, axis), part)  3.84 us
  transfers between devices with their start and end apart: 4, of which 3 were waited for; matrix products, arithmetic and copies ran while one was open for 27% of the time, Pallas kernels for 0%

commit v1 on v0

v1 whole, which is shorter than its diff:
```python
import functools

import jax
import jax.numpy as jnp
from jax import lax
from jax.experimental import pallas as pl
from jax.experimental.pallas import tpu as pltpu
from jax.sharding import PartitionSpec as P

MESH = pl.DeviceIdType.MESH
PAD = 8


def dot(left, right):
    return jnp.dot(left, right, preferred_element_type=jnp.float32)


def halves(x):
    hi = x.astype(jnp.bfloat16)
    lo = (x - hi.astype(jnp.float32)).astype(jnp.bfloat16)
    return hi, lo


def stacked(x):
    hi = x.astype(jnp.bfloat16).astype(jnp.float32)
    return jnp.concatenate([hi, x - hi], axis=0).astype(jnp.bfloat16)


def folded(r):
    rows = r.shape[0] // 2
    return r[:rows] + r[rows:]


def kernel(
    blocks, steps, rows, series,
    a_ref, g_ref, drive_ref, dyn_ref, init_ref, filt_ref, smooth_ref,
    a_full, g_full, a_pre, g_pre, vst, fst, lst, pst, dyn_hl, x_out, x_in, s_out, s_in,
    local_sem, send_sem, recv_sem, chain_send, chain_recv,
):
    dim = dyn_ref.shape[0]
    place = lax.axis_index("tm")
    me = lax.axis_index("col")
    sib = me + 1 - 2 * lax.rem(me, 2)
    cross = lax.rem(me + 2, 4)
    first = place == 0
    last = place == blocks - 1

    barrier = pltpu.get_barrier_semaphore()
    for other in (sib, cross):
        pl.semaphore_signal(barrier, inc=1, device_id={"col": other}, device_id_type=MESH)

    @pl.when(jnp.logical_not(first))
    def _():
        pl.semaphore_signal(barrier, inc=1, device_id={"tm": place - 1}, device_id_type=MESH)

    @pl.when(jnp.logical_not(last))
    def _():
        pl.semaphore_signal(barrier, inc=1, device_id={"tm": place + 1}, device_id_type=MESH)

    neighbours = 4 - jnp.where(first, 1, 0) - jnp.where(last, 1, 0)
    pl.semaphore_wait(barrier, neighbours)

    own = pl.ds(pl.multiple_of(me * rows, rows), rows)
    passed = pl.ds(pl.multiple_of(cross * rows, rows), rows)

    def move(which, kind, t):
        source, full = ((a_ref, a_full), (g_ref, g_full))[which]
        if kind == 2:
            src = full.at[t, passed, :]
            dst = full.at[t, passed, :]
        else:
            src = source.at[t]
            dst = full.at[t, own, :]
        return pltpu.make_async_remote_copy(
            src_ref=src,
            dst_ref=dst,
            send_sem=send_sem.at[which, kind, t],
            recv_sem=recv_sem.at[which, kind, t],
            device_id={"col": cross if kind == 1 else sib},
            device_id_type=MESH,
        )

    def kept(which):
        source, full = ((a_ref, a_full), (g_ref, g_full))[which]
        return pltpu.make_async_copy(source, full.at[:, own, :], local_sem.at[which])

    for t in range(steps):
        move(0, 1, t).start()
    for t in range(steps):
        move(0, 0, t).start()
    kept(0).start()

    hi, lo = halves(dyn_ref[...])
    dyn_hl[0] = hi
    dyn_hl[1] = lo
    rest = jnp.zeros((PAD - series, dim), jnp.float32)

    def padded(x):
        return jnp.concatenate([x, rest], axis=0)

    def pass_on(which, t):
        move(which, 1, t).wait_recv()
        move(which, 2, t).start()

    def keep_pre(pre, t, p):
        hi, lo = halves(p)
        pre[t, 0:dim] = hi
        pre[t, dim : 2 * dim] = lo

    kept(0).wait()
    ahead = 2
    for t in range(ahead):
        pass_on(0, t)

    def arrived(which, t):
        move(which, 0, t).wait_recv()
        move(which, 2, t).wait_recv()

    arrived(0, 0)
    a_pre[0, 0:dim] = a_full[0]
    a_pre[0, dim : 2 * dim] = jnp.zeros((dim, dim), jnp.bfloat16)
    v0 = padded(drive_ref[0])
    vst[0] = v0
    a_pre[0, 2 * dim : 2 * dim + 2 * PAD] = stacked(v0)

    def forward_step(t, carry):
        @pl.when(t + ahead - 1 < steps)
        def _():
            pass_on(0, t + ahead - 1)

        arrived(0, t)
        r = dot(a_pre[t - 1], a_full[t])
        v = folded(r[2 * dim :]) + padded(drive_ref[t])
        keep_pre(a_pre, t, r[0:dim] + r[dim : 2 * dim])
        vst[t] = v
        a_pre[t, 2 * dim : 2 * dim + 2 * PAD] = stacked(v)
        return carry

    lax.fori_loop(1, steps, forward_step, 0)

    for t in reversed(range(steps)):
        move(1, 1, t).start()
    for t in reversed(range(steps)):
        move(1, 0, t).start()
    kept(1).start()

    late = place >= blocks // 2

    def pass_gains():
        for t in reversed(range(steps)):
            pass_on(1, t)

    pl.when(late)(pass_gains)

    def chain(way):
        src, dst = ((x_out, x_in), (s_out, s_in))[way]
        return pltpu.make_async_remote_copy(
            src_ref=src,
            dst_ref=dst,
            send_sem=chain_send.at[way],
            recv_sem=chain_recv.at[way],
            device_id={"tm": place + 1 if way == 0 else place - 1},
            device_id_type=MESH,
        )

    @pl.when(first)
    def _():
        x_in[...] = padded(init_ref[...])

    @pl.when(jnp.logical_not(first))
    def _():
        chain(0).wait_recv()

    x = stacked(x_in[...])

    def filtered_at(t):
        r = dot(x, a_pre[t, 0:dim]) + dot(x, a_pre[t, dim : 2 * dim])
        f = folded(r) + vst[t]
        fst[t * PAD : (t + 1) * PAD] = f
        filt_ref[t] = f[0:series]
        return f

    x_out[...] = filtered_at(steps - 1)

    @pl.when(jnp.logical_not(last))
    def _():
        chain(0).start()

    for t in range(steps - 1):
        filtered_at(t)

    pl.when(jnp.logical_not(late))(pass_gains)

    f_all = stacked(fst[...])
    pst[...] = folded(dot(f_all, dyn_hl[0]) + dot(f_all, dyn_hl[1]))
    kept(1).wait()

    end = steps - 1

    def rows_of(t):
        return pl.ds(pl.multiple_of(t * PAD, PAD), PAD)

    arrived(1, end)

    @pl.when(last)
    def _():
        lst[end] = fst[rows_of(end)]

        def only_means(lap, state):
            t = end - lap
            arrived(1, t)
            now = folded(dot(stacked(state - pst[rows_of(t)]), g_full[t])) + fst[rows_of(t)]
            lst[t] = now
            return now

        lax.fori_loop(1, steps, only_means, fst[rows_of(end)])
        s_out[...] = lst[0]
        chain(1).start()
        for t in range(steps):
            smooth_ref[t] = lst[t][0:series]

    @pl.when(jnp.logical_not(last))
    def _():
        g_pre[end, 0:dim] = g_full[end]
        g_pre[end, dim : 2 * dim] = jnp.zeros((dim, dim), jnp.bfloat16)
        now = folded(dot(stacked(-pst[rows_of(end)]), g_full[end])) + fst[rows_of(end)]
        lst[end] = now
        g_pre[end, 2 * dim :] = stacked(now - pst[rows_of(end - 1)])

        def backward_step(lap, carry):
            t = end - lap
            arrived(1, t)
            r = dot(g_pre[t + 1], g_full[t])
            keep_pre(g_pre, t, r[0:dim] + r[dim : 2 * dim])
            now = folded(r[2 * dim :]) + fst[rows_of(t)]
            lst[t] = now
            below = jnp.maximum(t - 1, 0)
            g_pre[t, 2 * dim :] = stacked(now - pst[rows_of(below)])
            return carry

        lax.fori_loop(1, steps, backward_step, 0)

        chain(1).wait_recv()
        s = stacked(s_in[...])

        def smoothed_at(t):
            r = dot(s, g_pre[t, 0:dim]) + dot(s, g_pre[t, dim : 2 * dim])
            now = folded(r) + lst[t]
            smooth_ref[t] = now[0:series]
            return now

        s_out[...] = smoothed_at(0)

        @pl.when(jnp.logical_not(first))
        def _():
            chain(1).start()

        for t in range(1, steps):
            smoothed_at(t)

    def sent(t, carry):
        for which in range(2):
            for kind in range(3):
                move(which, kind, t).wait_send()
        return carry

    lax.fori_loop(0, steps, sent, 0)

    @pl.when(jnp.logical_not(last))
    def _():
        chain(0).wait_send()

    @pl.when(jnp.logical_not(first))
    def _():
        chain(1).wait_send()


def local(blocks, transition, drive, smoother_gain, dynamics, initial_mean):
    steps, rows, dim = transition.shape
    series = initial_mean.shape[0]
    vmem = pl.BlockSpec(memory_space=pltpu.VMEM)
    hbm = pl.BlockSpec(memory_space=pl.ANY)
    full = pltpu.VMEM((steps, dim, dim), jnp.bfloat16)
    pre = pltpu.VMEM((steps, 2 * dim + 2 * PAD, dim), jnp.bfloat16)
    means = pltpu.VMEM((steps, PAD, dim), jnp.float32)
    flat = pltpu.VMEM((steps * PAD, dim), jnp.float32)
    one = pltpu.VMEM((PAD, dim), jnp.float32)
    out = jax.ShapeDtypeStruct(drive.shape, jnp.float32)
    return pl.pallas_call(
        functools.partial(kernel, blocks, steps, rows, series),
        out_shape=(out, out),
        in_specs=[hbm, hbm, vmem, vmem, vmem],
        out_specs=(vmem, vmem),
        scratch_shapes=[
            full, full, pre, pre, means, flat, means, flat,
            pltpu.VMEM((2, dim, dim), jnp.bfloat16),
            one, one, one, one,
            pltpu.SemaphoreType.DMA((2,)),
            pltpu.SemaphoreType.DMA((2, 3, steps)),
            pltpu.SemaphoreType.DMA((2, 3, steps)),
            pltpu.SemaphoreType.DMA((2,)),
            pltpu.SemaphoreType.DMA((2,)),
        ],
        compiler_params=pltpu.CompilerParams(
            collective_id=0, has_side_effects=True, vmem_limit_bytes=40 * 1024 * 1024
        ),
    )(transition, smoother_gain, drive, dynamics, initial_mean)


def solution(mesh):
    placed = (P("tm", "col", None), P("tm", "col", None), P("tm", "col", None), P(), P("col", None))
    return jax.shard_map(
        functools.partial(local, mesh.shape["tm"]),
        mesh=mesh,
        in_specs=placed,
        out_specs=(P("tm", "col", None), P("tm", "col", None)),
        check_vma=False,
    )
```

time: 172 us -> 64 us (0.37)
  blocking collectives: 65.3 us -> 0 us
  Pallas kernels: 0 us -> 57.5 us
  matrix products: 44.1 us -> 0 us
  waiting for transfers between devices: 38.1 us -> 0 us
  between operations: 14 us -> 0.65 us
  other arithmetic: 2.33 us -> 0 us
    all_gather x2 -> x0, blocking collectives: 65.3 us -> none  [prefix(): gathered = jax.tree.map(lambda a: lax.all_gather(a, axis), part)]
    pallas_call x0 -> x1, Pallas kernels: none -> 57.5 us  [local(): pl.pallas_call(functools.partial(kernel, blocks, steps, rows, series), ou...]
    dot_general x70 -> x0, matrix products: 44.1 us -> none  [product(): jnp.dot(left, right, precision=highest, preferred_element_type=jnp.float32)]
    all_gather x4 -> x0, waiting for transfers between devices: 36.7 us -> none  [the longest x1 20.3 us: local(): lax.all_gather(transition, 'col', axis=1, tiled=True)]
    all_gather x2 -> x0, local copies, waits for them, and re-layouts: 3.84 us -> none  [prefix(): gathered = jax.tree.map(lambda a: lax.all_gather(a, axis), part)]
    unnamed x10 -> x12, local copies, waits for them, and re-layouts: 2.08 us -> 5.52 us
  transfers between devices with their start and end apart: 4 -> 0, of which waited for: 3 -> 0; matrix products, arithmetic and copies ran while one was open for 27% -> 0% of each run, Pallas kernels for 0% -> 0%
where the time goes in v1:
time: 64 us; the launch traced here: 63.7 us
  Pallas kernels  57.5 us (90%)
  local copies, waits for them, and re-layouts  5.52 us (9%)
  between operations  0.65 us (1%)
    pallas_call x1, Pallas kernels, local(): pl.pallas_call(functools.partial(kernel, blocks, steps, rows, series), ou...  57.5 us
    unnamed x12, local copies, waits for them, and re-layouts  5.52 us

profile of v1, /device:TPU:0, one launch (start us, length us, event | category | flops | bytes accessed | tf_op | source)
XLA Modules:
  0.0 63.7 jit_solution(15476197639899364400)
XLA Ops:
  0.6 0.0 copy-start
  0.6 0.9 %copy-done = bf16[8,64,256]{2,1,0:T(8,128)(2,1)S(1)} copy-done((bf16[8,64,256]{2,1,0:T(8,128)(2,1)S(1)}, bf16[8,64,256]{2,1,0:T(8,128)(2,1)}, u32[]{:S(2)}) %copy-start) | copy-done | bytes 262168
  1.6 0.0 copy-start.1
  1.6 0.9 %copy-done.1 = bf16[8,64,256]{2,1,0:T(8,128)(2,1)S(1)} copy-done((bf16[8,64,256]{2,1,0:T(8,128)(2,1)S(1)}, bf16[8,64,256]{2,1,0:T(8,128)(2,1)}, u32[]{:S(2)}) %copy-start.1) | copy-done | bytes 262168
  2.5 0.0 copy-start.2
  2.5 0.9 %copy-done.2 = f32[256,256]{1,0:T(8,128)S(1)} copy-done((f32[256,256]{1,0:T(8,128)S(1)}, f32[256,256]{1,0:T(8,128)}, u32[]{:S(2)}) %copy-start.2) | copy-done | bytes 262168
  3.5 0.0 copy-start.3
  3.5 0.8 %copy-done.3 = f32[8,4,256]{2,1,0:T(4,128)S(1)} copy-done((f32[8,4,256]{2,1,0:T(4,128)S(1)}, f32[8,4,256]{2,1,0:T(4,128)}, u32[]{:S(2)}) %copy-start.3) | copy-done | bytes 32792
  4.2 0.0 copy-start.4
  4.2 0.7 %copy-done.4 = f32[4,256]{1,0:T(4,128)S(1)} copy-done((f32[4,256]{1,0:T(4,128)S(1)}, f32[4,256]{1,0:T(4,128)}, u32[]{:S(2)}) %copy-start.4) | copy-done | bytes 4120
  4.9 57.5 %shard_map.68 = (f32[8,4,256]{2,1,0:T(4,128)S(1)}, f32[8,4,256]{2,1,0:T(4,128)S(1)}) custom-call(bf16[8,64,256]{2,1,0:T(8,128)(2,1)S(1)} %copy-done, bf16[8,64,256]{2,1,0:T(8,128)(2,1)S(1)} %copy-done.1, f32[8,4,256]{2,1,0:T(4,128)S(1)} %copy-done.3, f32[256,256]{1,0:T(8,128)S(1)} %copy-done.2, f32[4,256]{1,0:T(4,128)S(1)} %copy-done.4), custom_call_target="tpu_custom_call" | custom-call | tf_op jit(solution)/shard_map/pallas_call | solution.py:289
  62.4 0.6 copy.9
  63.0 0.6 copy.10
Async XLA Ops:
  0.6 1.0 %copy-start = (bf16[8,64,256]{2,1,0:T(8,128)(2,1)S(1)}, bf16[8,64,256]{2,1,0:T(8,128)(2,1)}, u32[]{:S(2)}) copy-start(bf16[8,64,256]{2,1,0:T(8,128)(2,1)} %a_ref.1) | copy-start | bytes 786436
  1.6 0.9 %copy-start.1 = (bf16[8,64,256]{2,1,0:T(8,128)(2,1)S(1)}, bf16[8,64,256]{2,1,0:T(8,128)(2,1)}, u32[]{:S(2)}) copy-start(bf16[8,64,256]{2,1,0:T(8,128)(2,1)} %g_ref.1) | copy-start | bytes 786436
  2.5 0.9 %copy-start.2 = (f32[256,256]{1,0:T(8,128)S(1)}, f32[256,256]{1,0:T(8,128)}, u32[]{:S(2)}) copy-start(f32[256,256]{1,0:T(8,128)} %dyn_ref.1) | copy-start | bytes 786436
  3.5 0.8 %copy-start.3 = (f32[8,4,256]{2,1,0:T(4,128)S(1)}, f32[8,4,256]{2,1,0:T(4,128)}, u32[]{:S(2)}) copy-start(f32[8,4,256]{2,1,0:T(4,128)} %drive_ref.1) | copy-start | bytes 98308
  4.2 0.7 %copy-start.4 = (f32[4,256]{1,0:T(4,128)S(1)}, f32[4,256]{1,0:T(4,128)}, u32[]{:S(2)}) copy-start(f32[4,256]{1,0:T(4,128)} %init_ref.1) | copy-start | bytes 12292

commit v2 on v1

v2 whole, which is shorter than its diff:
```python
import functools

import jax
import jax.numpy as jnp
from jax import lax
from jax.experimental import pallas as pl
from jax.experimental.pallas import tpu as pltpu
from jax.sharding import PartitionSpec as P

MESH = pl.DeviceIdType.MESH
PAD = 8
GROUP = 4


def dot(left, right):
    return jnp.dot(left, right, preferred_element_type=jnp.float32)


def halves(x):
    hi = x.astype(jnp.bfloat16)
    lo = (x - hi.astype(jnp.float32)).astype(jnp.bfloat16)
    return hi, lo


def stacked(x):
    hi = x.astype(jnp.bfloat16).astype(jnp.float32)
    return jnp.concatenate([hi, x - hi], axis=0).astype(jnp.bfloat16)


def folded(r):
    rows = r.shape[0] // 2
    return r[:rows] + r[rows:]


def kernel(
    blocks, steps, rows, series,
    a_ref, g_ref, drive_hbm, dyn_hbm, init_hbm, filt_ref, smooth_ref,
    drive_ref, dyn_ref, init_ref,
    a_full, g_full, a_pre, g_pre, a_got, g_got, v_got, b_got, v_out, b_out,
    vst, fst, lst, pst, dyn_hl, x_out, x_in, s_out, s_in,
    local_sem, send_sem, recv_sem, group_send, group_recv, chain_send, chain_recv,
):
    dim = dyn_ref.shape[0]

    def fetch(n):
        src, dst = ((drive_hbm, drive_ref), (dyn_hbm, dyn_ref), (init_hbm, init_ref))[n]
        return pltpu.make_async_copy(src, dst, local_sem.at[2 + n])

    for n in range(3):
        fetch(n).start()
    place = lax.axis_index("tm")
    me = lax.axis_index("col")
    sib = me + 1 - 2 * lax.rem(me, 2)
    cross = lax.rem(me + 2, 4)
    q = lax.rem(place, GROUP)
    begin = place - q
    first = place == 0
    last = place == blocks - 1
    low = begin == 0
    high = begin == blocks - GROUP

    barrier = pltpu.get_barrier_semaphore()

    def greet(other):
        pl.semaphore_signal(barrier, inc=1, device_id=other, device_id_type=MESH)

    greet({"col": sib})
    greet({"col": cross})
    for d in range(1, GROUP):
        greet({"tm": begin + lax.rem(q + d, GROUP)})

    @pl.when(jnp.logical_not(high))
    def _():
        greet({"tm": begin + GROUP})

        @pl.when(q == GROUP - 1)
        def _():
            for d in range(1, GROUP):
                greet({"tm": begin + GROUP + d})

    @pl.when(jnp.logical_not(low))
    def _():
        greet({"tm": begin - 1})

        @pl.when(q == 0)
        def _():
            for d in range(1, GROUP):
                greet({"tm": begin - 1 - d})

    above = jnp.where(high, 0, jnp.where(q == GROUP - 1, GROUP, 1))
    below = jnp.where(low, 0, jnp.where(q == 0, GROUP, 1))
    pl.semaphore_wait(barrier, GROUP + 1 + above + below)

    own = pl.ds(pl.multiple_of(me * rows, rows), rows)
    passed = pl.ds(pl.multiple_of(cross * rows, rows), rows)

    def move(which, kind, t):
        source, full = ((a_ref, a_full), (g_ref, g_full))[which]
        if kind == 2:
            src = full.at[t, passed, :]
            dst = full.at[t, passed, :]
        else:
            src = source.at[t]
            dst = full.at[t, own, :]
        return pltpu.make_async_remote_copy(
            src_ref=src,
            dst_ref=dst,
            send_sem=send_sem.at[which, kind, t],
            recv_sem=recv_sem.at[which, kind, t],
            device_id={"col": cross if kind == 1 else sib},
            device_id_type=MESH,
        )

    def kept(which):
        source, full = ((a_ref, a_full), (g_ref, g_full))[which]
        return pltpu.make_async_copy(source, full.at[:, own, :], local_sem.at[which])

    for t in range(steps):
        move(0, 1, t).start()
    for t in range(steps):
        move(0, 0, t).start()
    kept(0).start()

    for n in range(3):
        fetch(n).wait()

    hi, lo = halves(dyn_ref[...])
    dyn_hl[0] = hi
    dyn_hl[1] = lo
    rest = jnp.zeros((PAD - series, dim), jnp.float32)

    def padded(x):
        return jnp.concatenate([x, rest], axis=0)

    def pass_on(which, t):
        move(which, 1, t).wait_recv()
        move(which, 2, t).start()

    def keep_pre(pre, t, p):
        hi, lo = halves(p)
        pre[t, 0:dim] = hi
        pre[t, dim : 2 * dim] = lo

    kept(0).wait()
    ahead = 2
    for t in range(ahead):
        pass_on(0, t)

    def arrived(which, t):
        move(which, 0, t).wait_recv()
        move(which, 2, t).wait_recv()

    arrived(0, 0)
    a_pre[0, 0:dim] = a_full[0]
    a_pre[0, dim : 2 * dim] = jnp.zeros((dim, dim), jnp.bfloat16)
    v0 = padded(drive_ref[0])
    vst[0] = v0
    a_pre[0, 2 * dim : 2 * dim + 2 * PAD] = stacked(v0)

    def forward_step(t, carry):
        @pl.when(t + ahead - 1 < steps)
        def _():
            pass_on(0, t + ahead - 1)

        arrived(0, t)
        r = dot(a_pre[t - 1], a_full[t])
        v = folded(r[2 * dim :]) + padded(drive_ref[t])
        keep_pre(a_pre, t, r[0:dim] + r[dim : 2 * dim])
        vst[t] = v
        a_pre[t, 2 * dim : 2 * dim + 2 * PAD] = stacked(v)
        return carry

    lax.fori_loop(1, steps, forward_step, 0)

    for t in reversed(range(steps)):
        move(1, 1, t).start()
    for t in reversed(range(steps)):
        move(1, 0, t).start()
    kept(1).start()

    half = lax.rem(me, 2)
    mine = pl.ds(pl.multiple_of(half * dim, dim), dim)

    def group_copy(way, kind, slot, d):
        pre, got, out, means = ((a_pre, a_got, v_out, v_got), (g_pre, g_got, b_out, b_got))[way]
        block = steps - 1 if way == 0 else 0
        if kind == 0:
            src, dst = pre.at[block, mine, :], got.at[slot, mine, :]
        elif kind == 1:
            src, dst = out, means.at[slot]
        else:
            src, dst = got.at[slot, mine, :], got.at[slot, mine, :]
        to = {"col": sib} if kind == 2 else {"tm": place + d if way == 0 else place - d}
        return pltpu.make_async_remote_copy(
            src_ref=src,
            dst_ref=dst,
            send_sem=group_send.at[way, kind, slot if kind == 2 else d - 1],
            recv_sem=group_recv.at[way, kind, slot],
            device_id=to,
            device_id_type=MESH,
        )

    def each_target(way, body):
        for d in reversed(range(1, GROUP)):
            pl.when(q + d <= GROUP - 1 if way == 0 else q >= d)(functools.partial(body, d))

    def spread(way, kind):
        slot = q if way == 0 else q - 1
        each_target(way, lambda d: group_copy(way, kind, slot, d).start())

    def each_source(way, body):
        for s in range(GROUP - 1) if way == 0 else reversed(range(GROUP - 1)):
            pl.when(q > s if way == 0 else q <= s)(functools.partial(body, s))

    def share(way):
        def one(s):
            group_copy(way, 0, s, 1).wait_recv()
            group_copy(way, 2, s, 1).start()

        if way == 0:
            each_source(way, one)
        else:
            for s in reversed(range(GROUP - 1)):
                there = jnp.logical_and(q <= s, jnp.logical_not(jnp.logical_and(high, s == GROUP - 2)))
                pl.when(there)(functools.partial(one, s))

    v_out[...] = vst[steps - 1]
    spread(0, 0)
    spread(0, 1)

    end = steps - 1

    def rows_of(t):
        return pl.ds(pl.multiple_of(t * PAD, PAD), PAD)

    def gains():
        for t in reversed(range(steps)):
            pass_on(1, t)
        kept(1).wait()
        arrived(1, end)

        @pl.when(jnp.logical_not(last))
        def _():
            g_pre[end, 0:dim] = g_full[end]
            g_pre[end, dim : 2 * dim] = jnp.zeros((dim, dim), jnp.bfloat16)

            def gain_step(lap, carry):
                t = end - lap
                arrived(1, t)
                r = dot(g_pre[t + 1], g_full[t])
                keep_pre(g_pre, t, r[0:dim] + r[dim : 2 * dim])
                return carry

            lax.fori_loop(1, steps, gain_step, 0)
            spread(1, 0)

        @pl.when(last)
        def _():
            def only_wait(lap, carry):
                arrived(1, end - lap)
                return carry

            lax.fori_loop(1, steps, only_wait, 0)

    share(0)
    pl.when(jnp.logical_not(low))(gains)

    def chain(way, d):
        src, dst = ((x_out, x_in), (s_out, s_in))[way]
        return pltpu.make_async_remote_copy(
            src_ref=src,
            dst_ref=dst,
            send_sem=chain_send.at[way, d - 1],
            recv_sem=chain_recv.at[way],
            device_id={"tm": place + d if way == 0 else place - d},
            device_id_type=MESH,
        )

    def applied(state, pre, block):
        r = dot(state, pre[block, 0:dim]) + dot(state, pre[block, dim : 2 * dim])
        return folded(r)

    @pl.when(low)
    def _():
        x_in[...] = padded(init_ref[...])

    @pl.when(jnp.logical_not(low))
    def _():
        chain(0, 1).wait_recv()

    def take(s):
        group_copy(0, 2, s, 1).wait_recv()
        group_copy(0, 1, s, 1).wait_recv()
        x_in[...] = applied(stacked(x_in[...]), a_got, s) + v_got[s]

    each_source(0, take)
    x = stacked(x_in[...])

    def filtered_at(t):
        f = applied(x, a_pre, t) + vst[t]
        fst[t * PAD : (t + 1) * PAD] = f
        filt_ref[t] = f[0:series]
        return f

    x_out[...] = filtered_at(end)
    gives = jnp.logical_and(q == GROUP - 1, jnp.logical_not(high))

    @pl.when(gives)
    def _():
        for d in reversed(range(1, GROUP + 1)):
            chain(0, d).start()

    for t in range(end):
        filtered_at(t)

    pl.when(low)(gains)

    f_all = stacked(fst[...])
    pst[...] = folded(dot(f_all, dyn_hl[0]) + dot(f_all, dyn_hl[1]))

    def mean_step(state, t):
        now = folded(dot(stacked(state - pst[rows_of(t)]), g_full[t])) + fst[rows_of(t)]
        lst[t] = now
        return now

    @pl.when(last)
    def _():
        lst[end] = fst[rows_of(end)]

    @pl.when(jnp.logical_not(last))
    def _():
        mean_step(jnp.zeros((PAD, dim), jnp.float32), end)

    state = lst[end]
    for t in reversed(range(end)):
        state = mean_step(state, t)
    b_out[...] = state
    spread(1, 1)
    share(1)

    @pl.when(high)
    def _():
        s_in[...] = jnp.zeros((PAD, dim), jnp.float32)

    @pl.when(jnp.logical_not(high))
    def _():
        chain(1, 1).wait_recv()

    def take_back(s):
        group_copy(1, 1, s, 1).wait_recv()

        def product():
            group_copy(1, 2, s, 1).wait_recv()
            s_in[...] = applied(stacked(s_in[...]), g_got, s) + b_got[s]

        if s == GROUP - 2:
            pl.when(jnp.logical_not(high))(product)

            @pl.when(high)
            def _():
                s_in[...] = b_got[s]
        else:
            product()

    each_source(1, take_back)

    @pl.when(last)
    def _():
        s_out[...] = lst[0]
        for t in range(steps):
            smooth_ref[t] = lst[t][0:series]

    returns = jnp.logical_and(q == 0, jnp.logical_not(low))

    @pl.when(jnp.logical_not(last))
    def _():
        s = stacked(s_in[...])

        def smoothed_at(t):
            now = applied(s, g_pre, t) + lst[t]
            smooth_ref[t] = now[0:series]
            return now

        s_out[...] = smoothed_at(0)

        @pl.when(returns)
        def _():
            for d in reversed(range(1, GROUP + 1)):
                chain(1, d).start()

        for t in range(1, steps):
            smoothed_at(t)

    def sent(t, carry):
        for which in range(2):
            for kind in range(3):
                move(which, kind, t).wait_send()
        return carry

    lax.fori_loop(0, steps, sent, 0)

    for way in range(2):
        for kind in range(2):
            def done(d, way=way, kind=kind):
                group_copy(way, kind, 0, d).wait_send()

            if way == 1 and kind == 0:
                pl.when(jnp.logical_not(last))(lambda: each_target(way, done))
            else:
                each_target(way, done)

    def shared(way, s):
        group_copy(way, 2, s, 1).wait_send()

    each_source(0, functools.partial(shared, 0))
    for s in range(GROUP - 1):
        there = jnp.logical_and(q <= s, jnp.logical_not(jnp.logical_and(high, s == GROUP - 2)))
        pl.when(there)(functools.partial(shared, 1, s))

    for way, sender in ((0, gives), (1, returns)):
        @pl.when(sender)
        def _():
            for d in range(1, GROUP + 1):
                chain(way, d).wait_send()


def local(blocks, transition, drive, smoother_gain, dynamics, initial_mean):
    steps, rows, dim = transition.shape
    series = initial_mean.shape[0]
    vmem = pl.BlockSpec(memory_space=pltpu.VMEM)
    hbm = pl.BlockSpec(memory_space=pltpu.HBM)
    full = pltpu.VMEM((steps, dim, dim), jnp.bfloat16)
    a_pre = pltpu.VMEM((steps, 2 * dim + 2 * PAD, dim), jnp.bfloat16)
    g_pre = pltpu.VMEM((steps, 2 * dim, dim), jnp.bfloat16)
    got = pltpu.VMEM((GROUP - 1, 2 * dim, dim), jnp.bfloat16)
    group = pltpu.VMEM((GROUP - 1, PAD, dim), jnp.float32)
    means = pltpu.VMEM((steps, PAD, dim), jnp.float32)
    flat = pltpu.VMEM((steps * PAD, dim), jnp.float32)
    one = pltpu.VMEM((PAD, dim), jnp.float32)
    out = jax.ShapeDtypeStruct(drive.shape, jnp.float32)
    return pl.pallas_call(
        functools.partial(kernel, blocks, steps, rows, series),
        out_shape=(out, out),
        in_specs=[hbm] * 5,
        out_specs=(vmem, vmem),
        scratch_shapes=[
            pltpu.VMEM(drive.shape, drive.dtype),
            pltpu.VMEM(dynamics.shape, dynamics.dtype),
            pltpu.VMEM(initial_mean.shape, initial_mean.dtype),
            full, full, a_pre, g_pre, got, got, group, group, one, one,
            means, flat, means, flat,
            pltpu.VMEM((2, dim, dim), jnp.bfloat16),
            one, one, one, one,
            pltpu.SemaphoreType.DMA((5,)),
            pltpu.SemaphoreType.DMA((2, 3, steps)),
            pltpu.SemaphoreType.DMA((2, 3, steps)),
            pltpu.SemaphoreType.DMA((2, 3, GROUP - 1)),
            pltpu.SemaphoreType.DMA((2, 3, GROUP - 1)),
            pltpu.SemaphoreType.DMA((2, GROUP)),
            pltpu.SemaphoreType.DMA((2,)),
        ],
        compiler_params=pltpu.CompilerParams(
            collective_id=0, has_side_effects=True, vmem_limit_bytes=60 * 1024 * 1024
        ),
    )(transition, smoother_gain, drive, dynamics, initial_mean)


def solution(mesh):
    placed = (P("tm", "col", None), P("tm", "col", None), P("tm", "col", None), P(), P("col", None))
    return jax.shard_map(
        functools.partial(local, mesh.shape["tm"]),
        mesh=mesh,
        in_specs=placed,
        out_specs=(P("tm", "col", None), P("tm", "col", None)),
        check_vma=False,
    )
```

time: 64 us -> 43 us (0.67)
  Pallas kernels: 57.5 us -> 40.1 us
  local copies, waits for them, and re-layouts: 5.52 us -> 2 us
    pallas_call x1, Pallas kernels: 57.5 us -> 40.1 us  [local(): pl.pallas_call(functools.partial(kernel, blocks, steps, rows, series), ou...]
    unnamed x12 -> x4, local copies, waits for them, and re-layouts: 5.52 us -> 2 us
where the time goes in v2:
time: 43 us; the launch traced here: 42.8 us
  Pallas kernels  40.1 us (93%)
  local copies, waits for them, and re-layouts  2 us (5%)
  between operations  0.65 us (2%)
    pallas_call x1, Pallas kernels, local(): pl.pallas_call(functools.partial(kernel, blocks, steps, rows, series), ou...  40.1 us
    unnamed x4, local copies, waits for them, and re-layouts  2 us

profile of v2, /device:TPU:0, one launch (start us, length us, event | category | flops | bytes accessed | tf_op | source)
XLA Modules:
  0.0 42.8 jit_solution(7361283131613009585)
XLA Ops:
  0.6 40.1 %shard_map.68 = (f32[8,4,256]{2,1,0:T(4,128)}, f32[8,4,256]{2,1,0:T(4,128)}) custom-call(bf16[8,64,256]{2,1,0:T(8,128)(2,1)} %a_ref.1, bf16[8,64,256]{2,1,0:T(8,128)(2,1)} %g_ref.1, f32[8,4,256]{2,1,0:T(4,128)} %drive_hbm.1, f32[256,256]{1,0:T(8,128)} %dyn_hbm.1, f32[4,256]{1,0:T(4,128)} %init_hbm.1), custom_call_target="tpu_custom_call" | custom-call | tf_op jit(solution)/shard_map/pallas_call | solution.py:441
  40.8 0.0 copy-start
  40.8 1.4 %copy.9 = f32[8,4,256]{2,1,0:T(4,128)} copy(f32[8,4,256]{2,1,0:T(4,128)} %get-tuple-element.4) | data formatting | bytes 65536
  42.2 0.0 copy-done
  42.2 0.6 %copy.10 = f32[8,4,256]{2,1,0:T(4,128)} copy(f32[8,4,256]{2,1,0:T(4,128)S(1)} %copy-done) | data formatting | bytes 65536
Async XLA Ops:
  40.8 1.4 %copy-start = (f32[8,4,256]{2,1,0:T(4,128)S(1)}, f32[8,4,256]{2,1,0:T(4,128)}, u32[]{:S(2)}) copy-start(f32[8,4,256]{2,1,0:T(4,128)} %get-tuple-element.5) | copy-start | bytes 98308

commit v3 on v2

--- a/solution.py
+++ b/solution.py
@@ -172,10 +172,14 @@
 
     lax.fori_loop(1, steps, forward_step, 0)
 
-    for t in reversed(range(steps)):
-        move(1, 1, t).start()
-    for t in reversed(range(steps)):
-        move(1, 0, t).start()
+    half_steps = steps // 2
+    laps = [(steps - 1 - n, half_steps - 1 - n) for n in range(half_steps)]
+    for pair in laps:
+        for t in pair:
+            move(1, 1, t).start()
+    for pair in laps:
+        for t in pair:
+            move(1, 0, t).start()
     kept(1).start()
 
     half = lax.rem(me, 2)
@@ -183,7 +187,7 @@
 
     def group_copy(way, kind, slot, d):
         pre, got, out, means = ((a_pre, a_got, v_out, v_got), (g_pre, g_got, b_out, b_got))[way]
-        block = steps - 1 if way == 0 else 0
+        block = steps - 1 if way == 0 else steps
         if kind == 0:
             src, dst = pre.at[block, mine, :], got.at[slot, mine, :]
         elif kind == 1:
@@ -212,20 +216,39 @@
         for s in range(GROUP - 1) if way == 0 else reversed(range(GROUP - 1)):
             pl.when(q > s if way == 0 else q <= s)(functools.partial(body, s))
 
+    def each_operator(way, body):
+        for s in range(GROUP - 1) if way == 0 else reversed(range(GROUP - 1)):
+            needed = q > s if way == 0 else q <= s
+            if way == 0 and s == 0:
+                needed = jnp.logical_and(needed, jnp.logical_not(low))
+            if way == 1 and s == GROUP - 2:
+                needed = jnp.logical_and(needed, jnp.logical_not(high))
+            pl.when(needed)(functools.partial(body, s))
+
     def share(way):
         def one(s):
             group_copy(way, 0, s, 1).wait_recv()
             group_copy(way, 2, s, 1).start()
 
-        if way == 0:
-            each_source(way, one)
-        else:
-            for s in reversed(range(GROUP - 1)):
-                there = jnp.logical_and(q <= s, jnp.logical_not(jnp.logical_and(high, s == GROUP - 2)))
-                pl.when(there)(functools.partial(one, s))
-
-    v_out[...] = vst[steps - 1]
-    spread(0, 0)
+        each_operator(way, one)
+
+    def applied(state, pre, block):
+        r = dot(state, pre[block, 0:dim]) + dot(state, pre[block, dim : 2 * dim])
+        return folded(r)
+
+    @pl.when(low)
+    def _():
+        x_in[...] = padded(init_ref[...])
+
+    @pl.when(first)
+    def _():
+        v_out[...] = applied(stacked(x_in[...]), a_pre, steps - 1) + vst[steps - 1]
+
+    @pl.when(jnp.logical_not(first))
+    def _():
+        v_out[...] = vst[steps - 1]
+        spread(0, 0)
+
     spread(0, 1)
 
     end = steps - 1
@@ -234,36 +257,38 @@
         return pl.ds(pl.multiple_of(t * PAD, PAD), PAD)
 
     def gains():
-        for t in reversed(range(steps)):
-            pass_on(1, t)
+        def pass_pair(n):
+            for t in laps[n]:
+                pass_on(1, t)
+
+        pass_pair(0)
+        pass_pair(1)
         kept(1).wait()
-        arrived(1, end)
+        for n, pair in enumerate(laps):
+            if 1 <= n < half_steps - 1:
+                pass_pair(n + 1)
+            for t in pair:
+                arrived(1, t)
+                if n == 0:
+                    g_pre[t, 0:dim] = g_full[t]
+                    g_pre[t, dim : 2 * dim] = jnp.zeros((dim, dim), jnp.bfloat16)
+                else:
+                    r = dot(g_pre[t + 1], g_full[t])
+                    keep_pre(g_pre, t, r[0:dim] + r[dim : 2 * dim])
 
         @pl.when(jnp.logical_not(last))
         def _():
-            g_pre[end, 0:dim] = g_full[end]
-            g_pre[end, dim : 2 * dim] = jnp.zeros((dim, dim), jnp.bfloat16)
-
-            def gain_step(lap, carry):
-                t = end - lap
-                arrived(1, t)
-                r = dot(g_pre[t + 1], g_full[t])
-                keep_pre(g_pre, t, r[0:dim] + r[dim : 2 * dim])
-                return carry
-
-            lax.fori_loop(1, steps, gain_step, 0)
+            r = dot(g_pre[half_steps], g_pre[0, 0:dim])
+            more = dot(g_pre[half_steps, 0:dim], g_pre[0, dim : 2 * dim])
+            keep_pre(g_pre, steps, r[0:dim] + r[dim : 2 * dim] + more)
             spread(1, 0)
 
-        @pl.when(last)
-        def _():
-            def only_wait(lap, carry):
-                arrived(1, end - lap)
-                return carry
-
-            lax.fori_loop(1, steps, only_wait, 0)
-
-    share(0)
-    pl.when(jnp.logical_not(low))(gains)
+    pl.when(low)(functools.partial(share, 0))
+
+    @pl.when(jnp.logical_not(low))
+    def _():
+        gains()
+        share(0)
 
     def chain(way, d):
         src, dst = ((x_out, x_in), (s_out, s_in))[way]
@@ -276,22 +301,25 @@
             device_id_type=MESH,
         )
 
-    def applied(state, pre, block):
-        r = dot(state, pre[block, 0:dim]) + dot(state, pre[block, dim : 2 * dim])
-        return folded(r)
-
-    @pl.when(low)
-    def _():
-        x_in[...] = padded(init_ref[...])
-
     @pl.when(jnp.logical_not(low))
     def _():
         chain(0, 1).wait_recv()
 
     def take(s):
-        group_copy(0, 2, s, 1).wait_recv()
         group_copy(0, 1, s, 1).wait_recv()
-        x_in[...] = applied(stacked(x_in[...]), a_got, s) + v_got[s]
+
+        def product():
+            group_copy(0, 2, s, 1).wait_recv()
+            x_in[...] = applied(stacked(x_in[...]), a_got, s) + v_got[s]
+
+        if s == 0:
+            pl.when(jnp.logical_not(low))(product)
+
+            @pl.when(low)
+            def _():
+                x_in[...] = v_got[s]
+        else:
+            product()
 
     each_source(0, take)
     x = stacked(x_in[...])
@@ -319,22 +347,19 @@
     pst[...] = folded(dot(f_all, dyn_hl[0]) + dot(f_all, dyn_hl[1]))
 
     def mean_step(state, t):
-        now = folded(dot(stacked(state - pst[rows_of(t)]), g_full[t])) + fst[rows_of(t)]
+        moved = -pst[rows_of(t)] if state is None else state - pst[rows_of(t)]
+        now = folded(dot(stacked(moved), g_full[t]))
+        if t == end:
+            now = jnp.where(last, jnp.zeros_like(now), now)
+        now = now + fst[rows_of(t)]
         lst[t] = now
         return now
 
-    @pl.when(last)
-    def _():
-        lst[end] = fst[rows_of(end)]
-
-    @pl.when(jnp.logical_not(last))
-    def _():
-        mean_step(jnp.zeros((PAD, dim), jnp.float32), end)
-
-    state = lst[end]
-    for t in reversed(range(end)):
-        state = mean_step(state, t)
-    b_out[...] = state
+    upper = lower = None
+    for t_up, t_low in laps:
+        upper = mean_step(upper, t_up)
+        lower = mean_step(lower, t_low)
+    b_out[...] = applied(stacked(upper), g_pre, 0) + lower
     spread(1, 1)
     share(1)
 
@@ -364,32 +389,35 @@
 
     each_source(1, take_back)
 
+    returns = jnp.logical_and(q == 0, jnp.logical_not(low))
+
     @pl.when(last)
     def _():
-        s_out[...] = lst[0]
-        for t in range(steps):
+        smooth_ref[0] = b_out[0:series]
+        for t in range(half_steps, steps):
             smooth_ref[t] = lst[t][0:series]
 
-    returns = jnp.logical_and(q == 0, jnp.logical_not(low))
-
     @pl.when(jnp.logical_not(last))
     def _():
         s = stacked(s_in[...])
-
-        def smoothed_at(t):
+        now = applied(s, g_pre, steps) + b_out[...]
+        s_out[...] = now
+        smooth_ref[0] = now[0:series]
+
+        @pl.when(returns)
+        def _():
+            for d in reversed(range(1, GROUP + 1)):
+                chain(1, d).start()
+
+        for t in range(half_steps, steps):
             now = applied(s, g_pre, t) + lst[t]
             smooth_ref[t] = now[0:series]
-            return now
-
-        s_out[...] = smoothed_at(0)
-
-        @pl.when(returns)
-        def _():
-            for d in reversed(range(1, GROUP + 1)):
-                chain(1, d).start()
-
-        for t in range(1, steps):
-            smoothed_at(t)
+            if t == half_steps:
+                lst[t] = now
+
+    middle = stacked(lst[half_steps])
+    for t in range(1, half_steps):
+        smooth_ref[t] = (applied(middle, g_pre, t) + lst[t])[0:series]
 
     def sent(t, carry):
         for which in range(2):
@@ -399,23 +427,17 @@
 
     lax.fori_loop(0, steps, sent, 0)
 
-    for way in range(2):
-        for kind in range(2):
-            def done(d, way=way, kind=kind):
-                group_copy(way, kind, 0, d).wait_send()
-
-            if way == 1 and kind == 0:
-                pl.when(jnp.logical_not(last))(lambda: each_target(way, done))
-            else:
-                each_target(way, done)
-
-    def shared(way, s):
-        group_copy(way, 2, s, 1).wait_send()
-
-    each_source(0, functools.partial(shared, 0))
-    for s in range(GROUP - 1):
-        there = jnp.logical_and(q <= s, jnp.logical_not(jnp.logical_and(high, s == GROUP - 2)))
-        pl.when(there)(functools.partial(shared, 1, s))
+    for way, final in ((0, first), (1, last)):
+
+        def done(kind, d):
+            group_copy(way, kind, 0, d).wait_send()
+
+        @pl.when(jnp.logical_not(final))
+        def _():
+            each_target(way, functools.partial(done, 0))
+
+        each_target(way, functools.partial(done, 1))
+        each_operator(way, lambda s: group_copy(way, 2, s, 1).wait_send())
 
     for way, sender in ((0, gives), (1, returns)):
         @pl.when(sender)
@@ -431,7 +453,7 @@
     hbm = pl.BlockSpec(memory_space=pltpu.HBM)
     full = pltpu.VMEM((steps, dim, dim), jnp.bfloat16)
     a_pre = pltpu.VMEM((steps, 2 * dim + 2 * PAD, dim), jnp.bfloat16)
-    g_pre = pltpu.VMEM((steps, 2 * dim, dim), jnp.bfloat16)
+    g_pre = pltpu.VMEM((steps + 1, 2 * dim, dim), jnp.bfloat16)
     got = pltpu.VMEM((GROUP - 1, 2 * dim, dim), jnp.bfloat16)
     group = pltpu.VMEM((GROUP - 1, PAD, dim), jnp.float32)
     means = pltpu.VMEM((steps, PAD, dim), jnp.float32)

time: 43 us -> 42 us (0.977)
  Pallas kernels: 40.1 us -> 39.1 us
    pallas_call x1, Pallas kernels: 40.1 us -> 39.1 us  [local(): pl.pallas_call(functools.partial(kernel, blocks, steps, rows, series), ou...]
where the time goes in v3:
time: 42 us; the launch traced here: 41.8 us
  Pallas kernels  39.1 us (93%)
  local copies, waits for them, and re-layouts  2 us (5%)
  between operations  0.65 us (2%)
    pallas_call x1, Pallas kernels, local(): pl.pallas_call(functools.partial(kernel, blocks, steps, rows, series), ou...  39.1 us
    unnamed x4, local copies, waits for them, and re-layouts  2 us

profile of v3, /device:TPU:0, one launch (start us, length us, event | category | flops | bytes accessed | tf_op | source)
XLA Modules:
  0.0 41.8 jit_solution(14310848166042196127)
XLA Ops:
  0.6 39.1 %shard_map.68 = (f32[8,4,256]{2,1,0:T(4,128)}, f32[8,4,256]{2,1,0:T(4,128)}) custom-call(bf16[8,64,256]{2,1,0:T(8,128)(2,1)} %a_ref.1, bf16[8,64,256]{2,1,0:T(8,128)(2,1)} %g_ref.1, f32[8,4,256]{2,1,0:T(4,128)} %drive_hbm.1, f32[256,256]{1,0:T(8,128)} %dyn_hbm.1, f32[4,256]{1,0:T(4,128)} %init_hbm.1), custom_call_target="tpu_custom_call" | custom-call | tf_op jit(solution)/shard_map/pallas_call | solution.py:463
  39.8 0.0 copy-start
  39.8 1.4 %copy.9 = f32[8,4,256]{2,1,0:T(4,128)} copy(f32[8,4,256]{2,1,0:T(4,128)} %get-tuple-element.4) | data formatting | bytes 65536
  41.2 0.0 copy-done
  41.2 0.6 %copy.10 = f32[8,4,256]{2,1,0:T(4,128)} copy(f32[8,4,256]{2,1,0:T(4,128)S(1)} %copy-done) | data formatting | bytes 65536
Async XLA Ops:
  39.8 1.4 %copy-start = (f32[8,4,256]{2,1,0:T(4,128)S(1)}, f32[8,4,256]{2,1,0:T(4,128)}, u32[]{:S(2)}) copy-start(f32[8,4,256]{2,1,0:T(4,128)} %get-tuple-element.5) | copy-start | bytes 98308

commit v4 on v3

--- a/solution.py
+++ b/solution.py
@@ -36,7 +36,7 @@
     blocks, steps, rows, series,
     a_ref, g_ref, drive_hbm, dyn_hbm, init_hbm, filt_ref, smooth_ref,
     drive_ref, dyn_ref, init_ref,
-    a_full, g_full, a_pre, g_pre, a_got, g_got, v_got, b_got, v_out, b_out,
+    a_full, g_full, a_pre, g_pre, a_got, g_got, v_got, b_got, v_out, b_out, e_pre, e_vec,
     vst, fst, lst, pst, dyn_hl, x_out, x_in, s_out, s_in,
     local_sem, send_sem, recv_sem, group_send, group_recv, chain_send, chain_recv,
 ):
@@ -120,6 +120,12 @@
     for t in range(steps):
         move(0, 0, t).start()
     kept(0).start()
+    kept(1).start()
+    half_steps = steps // 2
+
+    def lap_steps(n):
+        return steps - 1 - n, half_steps - 1 - n
+
 
     for n in range(3):
         fetch(n).wait()
@@ -142,7 +148,7 @@
         pre[t, dim : 2 * dim] = lo
 
     kept(0).wait()
-    ahead = 2
+    ahead = 3
     for t in range(ahead):
         pass_on(0, t)
 
@@ -161,6 +167,12 @@
         @pl.when(t + ahead - 1 < steps)
         def _():
             pass_on(0, t + ahead - 1)
+
+        @pl.when(t >= steps - half_steps)
+        def _():
+            for g in lap_steps(t - (steps - half_steps)):
+                move(1, 1, g).start()
+                move(1, 0, g).start()
 
         arrived(0, t)
         r = dot(a_pre[t - 1], a_full[t])
@@ -171,16 +183,6 @@
         return carry
 
     lax.fori_loop(1, steps, forward_step, 0)
-
-    half_steps = steps // 2
-    laps = [(steps - 1 - n, half_steps - 1 - n) for n in range(half_steps)]
-    for pair in laps:
-        for t in pair:
-            move(1, 1, t).start()
-    for pair in laps:
-        for t in pair:
-            move(1, 0, t).start()
-    kept(1).start()
 
     half = lax.rem(me, 2)
     mine = pl.ds(pl.multiple_of(half * dim, dim), dim)
@@ -256,39 +258,41 @@
     def rows_of(t):
         return pl.ds(pl.multiple_of(t * PAD, PAD), PAD)
 
+    def joined(left, i, right, j):
+        r = dot(left[i, 0 : 2 * dim], right[j, 0:dim])
+        more = dot(left[i, 0:dim], right[j, dim : 2 * dim])
+        return r[0:dim] + r[dim : 2 * dim] + more
+
     def gains():
         def pass_pair(n):
-            for t in laps[n]:
+            for t in lap_steps(n):
                 pass_on(1, t)
 
         pass_pair(0)
         pass_pair(1)
         kept(1).wait()
-        for n, pair in enumerate(laps):
-            if 1 <= n < half_steps - 1:
+        for t in lap_steps(0):
+            arrived(1, t)
+            g_pre[t, 0:dim] = g_full[t]
+            g_pre[t, dim : 2 * dim] = jnp.zeros((dim, dim), jnp.bfloat16)
+
+        def lap(n, carry):
+            @pl.when(n < half_steps - 1)
+            def _():
                 pass_pair(n + 1)
-            for t in pair:
+
+            for t in lap_steps(n):
                 arrived(1, t)
-                if n == 0:
-                    g_pre[t, 0:dim] = g_full[t]
-                    g_pre[t, dim : 2 * dim] = jnp.zeros((dim, dim), jnp.bfloat16)
-                else:
-                    r = dot(g_pre[t + 1], g_full[t])
-                    keep_pre(g_pre, t, r[0:dim] + r[dim : 2 * dim])
+                r = dot(g_pre[t + 1], g_full[t])
+                keep_pre(g_pre, t, r[0:dim] + r[dim : 2 * dim])
+            return carry
+
+        lax.fori_loop(1, half_steps, lap, 0)
 
         @pl.when(jnp.logical_not(last))
         def _():
-            r = dot(g_pre[half_steps], g_pre[0, 0:dim])
-            more = dot(g_pre[half_steps, 0:dim], g_pre[0, dim : 2 * dim])
-            keep_pre(g_pre, steps, r[0:dim] + r[dim : 2 * dim] + more)
+            keep_pre(g_pre, steps, joined(g_pre, half_steps, g_pre, 0))
             spread(1, 0)
-
-    pl.when(low)(functools.partial(share, 0))
-
-    @pl.when(jnp.logical_not(low))
-    def _():
-        gains()
-        share(0)
 
     def chain(way, d):
         src, dst = ((x_out, x_in), (s_out, s_in))[way]
@@ -301,47 +305,56 @@
             device_id_type=MESH,
         )
 
-    @pl.when(jnp.logical_not(low))
-    def _():
-        chain(0, 1).wait_recv()
-
-    def take(s):
-        group_copy(0, 1, s, 1).wait_recv()
-
-        def product():
-            group_copy(0, 2, s, 1).wait_recv()
-            x_in[...] = applied(stacked(x_in[...]), a_got, s) + v_got[s]
-
-        if s == 0:
-            pl.when(jnp.logical_not(low))(product)
-
-            @pl.when(low)
-            def _():
-                x_in[...] = v_got[s]
-        else:
-            product()
-
-    each_source(0, take)
-    x = stacked(x_in[...])
-
-    def filtered_at(t):
-        f = applied(x, a_pre, t) + vst[t]
-        fst[t * PAD : (t + 1) * PAD] = f
-        filt_ref[t] = f[0:series]
-        return f
-
-    x_out[...] = filtered_at(end)
     gives = jnp.logical_and(q == GROUP - 1, jnp.logical_not(high))
 
-    @pl.when(gives)
-    def _():
-        for d in reversed(range(1, GROUP + 1)):
-            chain(0, d).start()
-
-    for t in range(end):
-        filtered_at(t)
-
-    pl.when(low)(gains)
+    def filtering():
+        share(0)
+
+        @pl.when(jnp.logical_not(low))
+        def _():
+            chain(0, 1).wait_recv()
+
+        def take(s):
+            group_copy(0, 1, s, 1).wait_recv()
+
+            def product():
+                group_copy(0, 2, s, 1).wait_recv()
+                x_in[...] = applied(stacked(x_in[...]), a_got, s) + v_got[s]
+
+            if s == 0:
+                pl.when(jnp.logical_not(low))(product)
+
+                @pl.when(low)
+                def _():
+                    x_in[...] = v_got[s]
+            else:
+                product()
+
+        each_source(0, take)
+        x = stacked(x_in[...])
+
+        def filtered_at(t):
+            f = applied(x, a_pre, t) + vst[t]
+            fst[t * PAD : (t + 1) * PAD] = f
+            filt_ref[t] = f[0:series]
+            return f
+
+        x_out[...] = filtered_at(end)
+
+        @pl.when(gives)
+        def _():
+            for d in reversed(range(1, GROUP + 1)):
+                chain(0, d).start()
+
+        for t in range(end):
+            filtered_at(t)
+
+    def phase(n, carry):
+        pl.when(low == (n == 1))(gains)
+        pl.when(n == 0)(filtering)
+        return carry
+
+    lax.fori_loop(0, 2, phase, 0)
 
     f_all = stacked(fst[...])
     pst[...] = folded(dot(f_all, dyn_hl[0]) + dot(f_all, dyn_hl[1]))
@@ -356,38 +369,47 @@
         return now
 
     upper = lower = None
-    for t_up, t_low in laps:
+    for t_up, t_low in map(lap_steps, range(half_steps)):
         upper = mean_step(upper, t_up)
         lower = mean_step(lower, t_low)
     b_out[...] = applied(stacked(upper), g_pre, 0) + lower
     spread(1, 1)
     share(1)
 
-    @pl.when(high)
-    def _():
-        s_in[...] = jnp.zeros((PAD, dim), jnp.float32)
-
-    @pl.when(jnp.logical_not(high))
-    def _():
-        chain(1, 1).wait_recv()
+    @pl.when(q == GROUP - 1)
+    def _():
+        e_vec[...] = jnp.zeros((PAD, dim), jnp.float32)
 
     def take_back(s):
         group_copy(1, 1, s, 1).wait_recv()
-
-        def product():
+        if s == GROUP - 2:
+            e_vec[...] = b_got[s]
+
+            @pl.when(jnp.logical_not(high))
+            def _():
+                group_copy(1, 2, s, 1).wait_recv()
+                e_pre[0] = g_got[s]
+        else:
             group_copy(1, 2, s, 1).wait_recv()
-            s_in[...] = applied(stacked(s_in[...]), g_got, s) + b_got[s]
-
-        if s == GROUP - 2:
-            pl.when(jnp.logical_not(high))(product)
-
-            @pl.when(high)
+            e_vec[...] = applied(stacked(e_vec[...]), g_got, s) + b_got[s]
+
+            @pl.when(jnp.logical_not(high))
             def _():
-                s_in[...] = b_got[s]
-        else:
-            product()
+                keep_pre(e_pre, 0, joined(e_pre, 0, g_got, s))
 
     each_source(1, take_back)
+
+    @pl.when(high)
+    def _():
+        s_in[...] = e_vec[...]
+
+    @pl.when(jnp.logical_not(high))
+    def _():
+        chain(1, 1).wait_recv()
+
+        @pl.when(q < GROUP - 1)
+        def _():
+            s_in[...] = applied(stacked(s_in[...]), e_pre, 0) + e_vec[...]
 
     returns = jnp.logical_and(q == 0, jnp.logical_not(low))
 
@@ -470,6 +492,7 @@
             pltpu.VMEM(dynamics.shape, dynamics.dtype),
             pltpu.VMEM(initial_mean.shape, initial_mean.dtype),
             full, full, a_pre, g_pre, got, got, group, group, one, one,
+            pltpu.VMEM((1, 2 * dim, dim), jnp.bfloat16), one,
             means, flat, means, flat,
             pltpu.VMEM((2, dim, dim), jnp.bfloat16),
             one, one, one, one,

time: 42 us -> 41.9 us (level)
  no operation moved by 1% of the time
where the time goes in v4:
time: 41.9 us; the launch traced here: 41.7 us
  Pallas kernels  39.1 us (93%)
  local copies, waits for them, and re-layouts  2 us (5%)
  between operations  0.65 us (2%)
    pallas_call x1, Pallas kernels, local(): pl.pallas_call(functools.partial(kernel, blocks, steps, rows, series), ou...  39.1 us
    unnamed x4, local copies, waits for them, and re-layouts  2 us

profile of v4, /device:TPU:0, one launch (start us, length us, event | category | flops | bytes accessed | tf_op | source)
XLA Modules:
  0.0 41.7 jit_solution(14348156719298142052)
XLA Ops:
  0.6 39.1 %shard_map.68 = (f32[8,4,256]{2,1,0:T(4,128)}, f32[8,4,256]{2,1,0:T(4,128)}) custom-call(bf16[8,64,256]{2,1,0:T(8,128)(2,1)} %a_ref.1, bf16[8,64,256]{2,1,0:T(8,128)(2,1)} %g_ref.1, f32[8,4,256]{2,1,0:T(4,128)} %drive_hbm.1, f32[256,256]{1,0:T(8,128)} %dyn_hbm.1, f32[4,256]{1,0:T(4,128)} %init_hbm.1), custom_call_target="tpu_custom_call" | custom-call | tf_op jit(solution)/shard_map/pallas_call | solution.py:485
  39.7 0.0 copy-start
  39.7 1.4 %copy.9 = f32[8,4,256]{2,1,0:T(4,128)} copy(f32[8,4,256]{2,1,0:T(4,128)} %get-tuple-element.4) | data formatting | bytes 65536
  41.1 0.0 copy-done
  41.1 0.6 %copy.10 = f32[8,4,256]{2,1,0:T(4,128)} copy(f32[8,4,256]{2,1,0:T(4,128)S(1)} %copy-done) | data formatting | bytes 65536
Async XLA Ops:
  39.7 1.4 %copy-start = (f32[8,4,256]{2,1,0:T(4,128)S(1)}, f32[8,4,256]{2,1,0:T(4,128)}, u32[]{:S(2)}) copy-start(f32[8,4,256]{2,1,0:T(4,128)} %get-tuple-element.5) | copy-start | bytes 98308

commit v5 on v4

--- a/solution.py
+++ b/solution.py
@@ -36,7 +36,7 @@
     blocks, steps, rows, series,
     a_ref, g_ref, drive_hbm, dyn_hbm, init_hbm, filt_ref, smooth_ref,
     drive_ref, dyn_ref, init_ref,
-    a_full, g_full, a_pre, g_pre, a_got, g_got, v_got, b_got, v_out, b_out, e_pre, e_vec,
+    a_full, g_full, a_pre, g_pre, a_got, g_got, v_got, b_got, v_out, b_out, e_pre, e_vec, d_pre, d_vec,
     vst, fst, lst, pst, dyn_hl, x_out, x_in, s_out, s_in,
     local_sem, send_sem, recv_sem, group_send, group_recv, chain_send, chain_recv,
 ):
@@ -310,27 +310,37 @@
     def filtering():
         share(0)
 
-        @pl.when(jnp.logical_not(low))
-        def _():
-            chain(0, 1).wait_recv()
-
         def take(s):
             group_copy(0, 1, s, 1).wait_recv()
-
-            def product():
+            if s == 0:
+                d_vec[...] = v_got[s]
+
+                @pl.when(jnp.logical_not(low))
+                def _():
+                    group_copy(0, 2, s, 1).wait_recv()
+                    d_pre[0] = a_got[s]
+            else:
                 group_copy(0, 2, s, 1).wait_recv()
-                x_in[...] = applied(stacked(x_in[...]), a_got, s) + v_got[s]
-
-            if s == 0:
-                pl.when(jnp.logical_not(low))(product)
-
-                @pl.when(low)
+                d_vec[...] = applied(stacked(d_vec[...]), a_got, s) + v_got[s]
+
+                @pl.when(jnp.logical_not(low))
                 def _():
-                    x_in[...] = v_got[s]
-            else:
-                product()
+                    keep_pre(d_pre, 0, joined(d_pre, 0, a_got, s))
 
         each_source(0, take)
+
+        @pl.when(jnp.logical_and(low, q > 0))
+        def _():
+            x_in[...] = d_vec[...]
+
+        @pl.when(jnp.logical_not(low))
+        def _():
+            chain(0, 1).wait_recv()
+
+            @pl.when(q > 0)
+            def _():
+                x_in[...] = applied(stacked(x_in[...]), d_pre, 0) + d_vec[...]
+
         x = stacked(x_in[...])
 
         def filtered_at(t):
@@ -349,8 +359,10 @@
         for t in range(end):
             filtered_at(t)
 
+    hurry = jnp.logical_and(low, q == GROUP - 1)
+
     def phase(n, carry):
-        pl.when(low == (n == 1))(gains)
+        pl.when(hurry == (n == 1))(gains)
         pl.when(n == 0)(filtering)
         return carry
 
@@ -493,6 +505,7 @@
             pltpu.VMEM(initial_mean.shape, initial_mean.dtype),
             full, full, a_pre, g_pre, got, got, group, group, one, one,
             pltpu.VMEM((1, 2 * dim, dim), jnp.bfloat16), one,
+            pltpu.VMEM((1, 2 * dim, dim), jnp.bfloat16), one,
             means, flat, means, flat,
             pltpu.VMEM((2, dim, dim), jnp.bfloat16),
             one, one, one, one,

time: 41.9 us -> 40.4 us (0.964)
  Pallas kernels: 39.1 us -> 37.6 us
    pallas_call x1, Pallas kernels: 39.1 us -> 37.6 us  [local(): pl.pallas_call(functools.partial(kernel, blocks, steps, rows, series), ou...]
where the time goes in v5:
time: 40.4 us; the launch traced here: 40.2 us
  Pallas kernels  37.6 us (93%)
  local copies, waits for them, and re-layouts  2 us (5%)
  between operations  0.65 us (2%)
    pallas_call x1, Pallas kernels, local(): pl.pallas_call(functools.partial(kernel, blocks, steps, rows, series), ou...  37.6 us
    unnamed x4, local copies, waits for them, and re-layouts  2 us

profile of v5, /device:TPU:0, one launch (start us, length us, event | category | flops | bytes accessed | tf_op | source)
XLA Modules:
  0.0 40.2 jit_solution(7511007306059427749)
XLA Ops:
  0.6 37.6 %shard_map.68 = (f32[8,4,256]{2,1,0:T(4,128)}, f32[8,4,256]{2,1,0:T(4,128)}) custom-call(bf16[8,64,256]{2,1,0:T(8,128)(2,1)} %a_ref.1, bf16[8,64,256]{2,1,0:T(8,128)(2,1)} %g_ref.1, f32[8,4,256]{2,1,0:T(4,128)} %drive_hbm.1, f32[256,256]{1,0:T(8,128)} %dyn_hbm.1, f32[4,256]{1,0:T(4,128)} %init_hbm.1), custom_call_target="tpu_custom_call" | custom-call | tf_op jit(solution)/shard_map/pallas_call | solution.py:497
  38.2 0.0 copy-start
  38.2 1.4 %copy.9 = f32[8,4,256]{2,1,0:T(4,128)} copy(f32[8,4,256]{2,1,0:T(4,128)} %get-tuple-element.4) | data formatting | bytes 65536
  39.6 0.0 copy-done
  39.6 0.6 %copy.10 = f32[8,4,256]{2,1,0:T(4,128)} copy(f32[8,4,256]{2,1,0:T(4,128)S(1)} %copy-done) | data formatting | bytes 65536
Async XLA Ops:
  38.2 1.4 %copy-start = (f32[8,4,256]{2,1,0:T(4,128)S(1)}, f32[8,4,256]{2,1,0:T(4,128)}, u32[]{:S(2)}) copy-start(f32[8,4,256]{2,1,0:T(4,128)} %get-tuple-element.5) | copy-start | bytes 98308

commit v6 on v5

--- a/solution.py
+++ b/solution.py
@@ -36,7 +36,7 @@
     blocks, steps, rows, series,
     a_ref, g_ref, drive_hbm, dyn_hbm, init_hbm, filt_ref, smooth_ref,
     drive_ref, dyn_ref, init_ref,
-    a_full, g_full, a_pre, g_pre, a_got, g_got, v_got, b_got, v_out, b_out, e_pre, e_vec, d_pre, d_vec,
+    a_full, g_full, a_pre, g_pre, a_got, g_got, v_got, b_got, v_out, b_out, e_pre, e_vec, d_pre, d_vec, u_pre,
     vst, fst, lst, pst, dyn_hl, x_out, x_in, s_out, s_in,
     local_sem, send_sem, recv_sem, group_send, group_recv, chain_send, chain_recv,
 ):
@@ -263,6 +263,9 @@
         more = dot(left[i, 0:dim], right[j, dim : 2 * dim])
         return r[0:dim] + r[dim : 2 * dim] + more
 
+    def slot_of(base, i):
+        return i - 1 + (0 if base == 0 else half_steps - 2)
+
     def gains():
         def pass_pair(n):
             for t in lap_steps(n):
@@ -293,6 +296,16 @@
         def _():
             keep_pre(g_pre, steps, joined(g_pre, half_steps, g_pre, 0))
             spread(1, 0)
+
+        for i in range(1, half_steps - 1):
+            for base in (half_steps, 0):
+                gain = g_full[base + i]
+                if i == 1:
+                    p = dot(gain, g_full[base])
+                else:
+                    n = slot_of(base, i - 1)
+                    p = dot(gain, u_pre[n, 0:dim]) + dot(gain, u_pre[n, dim : 2 * dim])
+                keep_pre(u_pre, slot_of(base, i), p)
 
     def chain(way, d):
         src, dst = ((x_out, x_in), (s_out, s_in))[way]
@@ -380,13 +393,31 @@
         lst[t] = now
         return now
 
+    def direct(base, top):
+        total = fst[rows_of(base)]
+        for i in range(half_steps):
+            less = pst[rows_of(base + i)]
+            if i < half_steps - 1:
+                moved = stacked(fst[rows_of(base + i + 1)] - less)
+                if i == 0:
+                    part = folded(dot(moved, g_full[base]))
+                else:
+                    part = applied(moved, u_pre, slot_of(base, i))
+            else:
+                part = applied(stacked(-less if top is None else top - less), g_pre, base)
+                if top is None:
+                    part = jnp.where(last, jnp.zeros_like(part), part)
+            total = total + part
+        return total
+
+    b_out[...] = direct(0, direct(half_steps, None))
+    spread(1, 1)
+    share(1)
+
     upper = lower = None
     for t_up, t_low in map(lap_steps, range(half_steps)):
         upper = mean_step(upper, t_up)
         lower = mean_step(lower, t_low)
-    b_out[...] = applied(stacked(upper), g_pre, 0) + lower
-    spread(1, 1)
-    share(1)
 
     @pl.when(q == GROUP - 1)
     def _():
@@ -494,6 +525,10 @@
     flat = pltpu.VMEM((steps * PAD, dim), jnp.float32)
     one = pltpu.VMEM((PAD, dim), jnp.float32)
     out = jax.ShapeDtypeStruct(drive.shape, jnp.float32)
+    pinned = [
+        pltpu.with_memory_space_constraint(x, pltpu.HBM)
+        for x in (transition, smoother_gain, drive, dynamics, initial_mean)
+    ]
     return pl.pallas_call(
         functools.partial(kernel, blocks, steps, rows, series),
         out_shape=(out, out),
@@ -506,6 +541,7 @@
             full, full, a_pre, g_pre, got, got, group, group, one, one,
             pltpu.VMEM((1, 2 * dim, dim), jnp.bfloat16), one,
             pltpu.VMEM((1, 2 * dim, dim), jnp.bfloat16), one,
+            pltpu.VMEM((steps - 4, 2 * dim, dim), jnp.bfloat16),
             means, flat, means, flat,
             pltpu.VMEM((2, dim, dim), jnp.bfloat16),
             one, one, one, one,
@@ -518,9 +554,9 @@
             pltpu.SemaphoreType.DMA((2,)),
         ],
         compiler_params=pltpu.CompilerParams(
-            collective_id=0, has_side_effects=True, vmem_limit_bytes=60 * 1024 * 1024
+            collective_id=0, has_side_effects=True, vmem_limit_bytes=40 * 1024 * 1024
         ),
-    )(transition, smoother_gain, drive, dynamics, initial_mean)
+    )(*pinned)
 
 
 def solution(mesh):

time: 40.4 us -> 39 us (0.965)
  local copies, waits for them, and re-layouts: 2 us -> 1.23 us
  Pallas kernels: 37.6 us -> 37 us
    unnamed x4 -> x2, local copies, waits for them, and re-layouts: 2 us -> 1.23 us
    pallas_call x1, Pallas kernels: 37.6 us -> 37 us  [local(): pl.pallas_call(functools.partial(kernel, blocks, steps, rows, series), ou...]
where the time goes in v6:
time: 39 us; the launch traced here: 38.8 us
  Pallas kernels  37 us (95%)
  local copies, waits for them, and re-layouts  1.23 us (3%)
  between operations  0.64 us (2%)
    pallas_call x1, Pallas kernels, local(): pl.pallas_call(functools.partial(kernel, blocks, steps, rows, series), ou...  37 us
    unnamed x2, local copies, waits for them, and re-layouts  1.23 us

profile of v6, /device:TPU:0, one launch (start us, length us, event | category | flops | bytes accessed | tf_op | source)
XLA Modules:
  0.0 38.8 jit_solution(5109674560335199722)
XLA Ops:
  0.6 37.0 %shard_map.68 = (f32[8,4,256]{2,1,0:T(4,128)S(1)}, f32[8,4,256]{2,1,0:T(4,128)S(1)}) custom-call(bf16[8,64,256]{2,1,0:T(8,128)(2,1)} %a_ref.1, bf16[8,64,256]{2,1,0:T(8,128)(2,1)} %g_ref.1, f32[8,4,256]{2,1,0:T(4,128)} %drive_hbm.1, f32[256,256]{1,0:T(8,128)} %dyn_hbm.1, f32[4,256]{1,0:T(4,128)} %init_hbm.1), custom_call_target="tpu_custom_call" | custom-call | tf_op jit(solution)/shard_map/pallas_call | solution.py:532
  37.6 0.6 %copy.9 = f32[8,4,256]{2,1,0:T(4,128)} copy(f32[8,4,256]{2,1,0:T(4,128)S(1)} %get-tuple-element.4) | data formatting | bytes 65536
  38.2 0.6 %copy.10 = f32[8,4,256]{2,1,0:T(4,128)} copy(f32[8,4,256]{2,1,0:T(4,128)S(1)} %get-tuple-element.5) | data formatting | bytes 65536

commit v7 on v6

--- a/solution.py
+++ b/solution.py
@@ -442,6 +442,29 @@
 
     each_source(1, take_back)
 
+    def settle():
+        def sent(t, carry):
+            for which in range(2):
+                for kind in range(3):
+                    move(which, kind, t).wait_send()
+            return carry
+
+        lax.fori_loop(0, steps, sent, 0)
+
+        for way, final in ((0, first), (1, last)):
+
+            def done(kind, d):
+                group_copy(way, kind, 0, d).wait_send()
+
+            @pl.when(jnp.logical_not(final))
+            def _():
+                each_target(way, functools.partial(done, 0))
+
+            each_target(way, functools.partial(done, 1))
+            each_operator(way, lambda s: group_copy(way, 2, s, 1).wait_send())
+
+    pl.when(low)(settle)
+
     @pl.when(high)
     def _():
         s_in[...] = e_vec[...]
@@ -484,25 +507,7 @@
     for t in range(1, half_steps):
         smooth_ref[t] = (applied(middle, g_pre, t) + lst[t])[0:series]
 
-    def sent(t, carry):
-        for which in range(2):
-            for kind in range(3):
-                move(which, kind, t).wait_send()
-        return carry
-
-    lax.fori_loop(0, steps, sent, 0)
-
-    for way, final in ((0, first), (1, last)):
-
-        def done(kind, d):
-            group_copy(way, kind, 0, d).wait_send()
-
-        @pl.when(jnp.logical_not(final))
-        def _():
-            each_target(way, functools.partial(done, 0))
-
-        each_target(way, functools.partial(done, 1))
-        each_operator(way, lambda s: group_copy(way, 2, s, 1).wait_send())
+    pl.when(jnp.logical_not(low))(settle)
 
     for way, sender in ((0, gives), (1, returns)):
         @pl.when(sender)

time: 39 us -> 39 us (level)
  no operation moved by 1% of the time
where the time goes in v7:
time: 39 us; the launch traced here: 38.8 us
  Pallas kernels  37 us (95%)
  local copies, waits for them, and re-layouts  1.23 us (3%)
  between operations  0.64 us (2%)
    pallas_call x1, Pallas kernels, local(): pl.pallas_call(functools.partial(kernel, blocks, steps, rows, series), ou...  37 us
    unnamed x2, local copies, waits for them, and re-layouts  1.23 us

profile of v7, /device:TPU:0, one launch (start us, length us, event | category | flops | bytes accessed | tf_op | source)
XLA Modules:
  0.0 38.8 jit_solution(13472242844909367518)
XLA Ops:
  0.6 37.0 %shard_map.68 = (f32[8,4,256]{2,1,0:T(4,128)S(1)}, f32[8,4,256]{2,1,0:T(4,128)S(1)}) custom-call(bf16[8,64,256]{2,1,0:T(8,128)(2,1)} %a_ref.1, bf16[8,64,256]{2,1,0:T(8,128)(2,1)} %g_ref.1, f32[8,4,256]{2,1,0:T(4,128)} %drive_hbm.1, f32[256,256]{1,0:T(8,128)} %dyn_hbm.1, f32[4,256]{1,0:T(4,128)} %init_hbm.1), custom_call_target="tpu_custom_call" | custom-call | tf_op jit(solution)/shard_map/pallas_call | solution.py:537
  37.6 0.6 %copy.9 = f32[8,4,256]{2,1,0:T(4,128)} copy(f32[8,4,256]{2,1,0:T(4,128)S(1)} %get-tuple-element.4) | data formatting | bytes 65536
  38.2 0.6 %copy.10 = f32[8,4,256]{2,1,0:T(4,128)} copy(f32[8,4,256]{2,1,0:T(4,128)S(1)} %get-tuple-element.5) | data formatting | bytes 65536

commit v8 on v7

--- a/solution.py
+++ b/solution.py
@@ -168,9 +168,9 @@
         def _():
             pass_on(0, t + ahead - 1)
 
-        @pl.when(t >= steps - half_steps)
-        def _():
-            for g in lap_steps(t - (steps - half_steps)):
+        @pl.when(jnp.logical_and(t >= 2, t < 2 + half_steps))
+        def _():
+            for g in lap_steps(t - 2):
                 move(1, 1, g).start()
                 move(1, 0, g).start()
 

time: 39 us -> 39 us (level)
  no operation moved by 1% of the time
where the time goes in v8:
time: 39 us; the launch traced here: 38.8 us
  Pallas kernels  37 us (95%)
  local copies, waits for them, and re-layouts  1.23 us (3%)
  between operations  0.64 us (2%)
    pallas_call x1, Pallas kernels, local(): pl.pallas_call(functools.partial(kernel, blocks, steps, rows, series), ou...  37 us
    unnamed x2, local copies, waits for them, and re-layouts  1.23 us

profile of v8, /device:TPU:0, one launch (start us, length us, event | category | flops | bytes accessed | tf_op | source)
XLA Modules:
  0.0 38.8 jit_solution(17993252197612014073)
XLA Ops:
  0.6 37.0 %shard_map.68 = (f32[8,4,256]{2,1,0:T(4,128)S(1)}, f32[8,4,256]{2,1,0:T(4,128)S(1)}) custom-call(bf16[8,64,256]{2,1,0:T(8,128)(2,1)} %a_ref.1, bf16[8,64,256]{2,1,0:T(8,128)(2,1)} %g_ref.1, f32[8,4,256]{2,1,0:T(4,128)} %drive_hbm.1, f32[256,256]{1,0:T(8,128)} %dyn_hbm.1, f32[4,256]{1,0:T(4,128)} %init_hbm.1), custom_call_target="tpu_custom_call" | custom-call | tf_op jit(solution)/shard_map/pallas_call | solution.py:537
  37.6 0.6 %copy.9 = f32[8,4,256]{2,1,0:T(4,128)} copy(f32[8,4,256]{2,1,0:T(4,128)S(1)} %get-tuple-element.4) | data formatting | bytes 65536
  38.2 0.6 %copy.10 = f32[8,4,256]{2,1,0:T(4,128)} copy(f32[8,4,256]{2,1,0:T(4,128)S(1)} %get-tuple-element.5) | data formatting | bytes 65536
